TPU v7x, 32 devices: a whole 2x2x4 slice. The times are simulated.
32 devices in a mesh: strip: 32 (over z, y, x, core).
Axes of the slice: x: 2, y: 2, z: 4, core: 2. Of those that a mesh axis runs over, the one named last changes fastest.
Arguments:
- params: float32 [59, 163840], P(None, 'strip'), may hold values from -23 to 23, as said below
- camera: float32 [4, 12], replicated, may hold values from -2 to 2, as said below
- send_index: int32 [1024, 320], P('strip'), may hold values from 0 to 5119, as said below
- send_count: int32 [1024], P('strip'), may hold values from 0 to 320, as said below
- tile_list: int32 [1280, 128], P('strip'), may hold values from 0 to 5119, as said below
- target: float32 [3, 512, 640], P(None, 'strip'), may hold values from 0 to 1
Outputs:
- param_grads: float32 [59, 163840], P(None, 'strip')
Inputs may be any that keep to these rules, and one draw needn't show every extreme that they name: `send_index`: in row s * 32 + r the first send_count[s * 32 + r] entries are distinct local Gaussian numbers of device s; over all r these live entries name each of device s's 5120 Gaussians exactly once. Later entries are local Gaussian numbers that name nothing sent. `send_count`: for every sender, and for every strip, the counts sum to 5120; the largest count equals 320. `tile_list`: each row holds 128 distinct received numbers of its strip; every number 0 to 5119 of a strip stands in exactly one of the strip's lists. `params`: each Gaussian lies 2 to 6 in front of the camera of the view of the strip that receives it and projects inside the tile whose list holds it; entry 6 of every Gaussian is 1 or more. `camera`: the first nine entries of each row form a rotation matrix.
All inputs are finite; a program needn't handle non-finite values.
Results may differ from a plain program's by a relative error of at most 0.0003.
Values sent between devices are 32-bit elements; how exact they have to be, the bound alone decides.
A program may use at most 64 MiB of HBM per device.

v0:
```python
import functools
import math

import jax
import jax.numpy as jnp
import numpy as np
from jax import lax
from jax.experimental import pallas as pl
from jax.experimental.pallas import tpu as pltpu
from jax.sharding import PartitionSpec as P

VIEWS = 4
FEET = 9
LANES = 128
LOG2E = math.log2(math.e)
NT = (((1,), (1,)), ((), ()))

exact_dot = lax.Precision.HIGHEST
harmonic_zero = 0.28209479177387814
harmonic_one = 0.4886025119029199
harmonic_two = (
    1.0925484305920792,
    -1.0925484305920792,
    0.31539156525252005,
    -1.0925484305920792,
    0.5462742152960396,
)
harmonic_three = (
    -0.5900435899266435,
    2.890611442640554,
    -0.4570457994644658,
    0.3731763325901154,
    -0.4570457994644658,
    1.445305721320277,
    -0.5900435899266435,
)
light_term = 0.0001
contrast_term = 0.0009


def harmonics(along_x, along_y, along_z):
    square_x = along_x * along_x
    square_y = along_y * along_y
    square_z = along_z * along_z
    return [
        harmonic_zero + 0.0 * along_x,
        -harmonic_one * along_y,
        harmonic_one * along_z,
        -harmonic_one * along_x,
        harmonic_two[0] * along_x * along_y,
        harmonic_two[1] * along_y * along_z,
        harmonic_two[2] * (2.0 * square_z - square_x - square_y),
        harmonic_two[3] * along_x * along_z,
        harmonic_two[4] * (square_x - square_y),
        harmonic_three[0] * along_y * (3.0 * square_x - square_y),
        harmonic_three[1] * along_x * along_y * along_z,
        harmonic_three[2] * along_y * (4.0 * square_z - square_x - square_y),
        harmonic_three[3] * along_z * (2.0 * square_z - 3.0 * square_x - 3.0 * square_y),
        harmonic_three[4] * along_x * (4.0 * square_z - square_x - square_y),
        harmonic_three[5] * along_z * (square_x - square_y),
        harmonic_three[6] * along_x * (square_x - 3.0 * square_y),
    ]


def project(params, camera, focal, centre_x, centre_y):
    rotation = [[camera[3 * row + col] for col in range(3)] for row in range(3)]
    mean = [params[axis] for axis in range(3)]
    placed = [
        rotation[row][0] * mean[0]
        + rotation[row][1] * mean[1]
        + rotation[row][2] * mean[2]
        + camera[9 + row]
        for row in range(3)
    ]
    depth = placed[2]
    inverse = 1.0 / depth
    screen_x = focal * placed[0] * inverse + centre_x
    screen_y = focal * placed[1] * inverse + centre_y
    quaternion = params[6:10]
    shrink = lax.rsqrt(sum(part * part for part in quaternion))
    real, imag_x, imag_y, imag_z = [part * shrink for part in quaternion]
    turn = [
        [
            1.0 - 2.0 * (imag_y * imag_y + imag_z * imag_z),
            2.0 * (imag_x * imag_y - real * imag_z),
            2.0 * (imag_x * imag_z + real * imag_y),
        ],
        [
            2.0 * (imag_x * imag_y + real * imag_z),
            1.0 - 2.0 * (imag_x * imag_x + imag_z * imag_z),
            2.0 * (imag_y * imag_z - real * imag_x),
        ],
        [
            2.0 * (imag_x * imag_z - real * imag_y),
            2.0 * (imag_y * imag_z + real * imag_x),
            1.0 - 2.0 * (imag_x * imag_x + imag_y * imag_y),
        ],
    ]
    scales = [jnp.exp(part) for part in params[3:6]]
    jacobian = [
        [focal * inverse, None, -focal * placed[0] * inverse * inverse],
        [None, focal * inverse, -focal * placed[1] * inverse * inverse],
    ]
    facing = [
        [
            jacobian[row][row] * rotation[row][col]
            + jacobian[row][2] * rotation[2][col]
            for col in range(3)
        ]
        for row in range(2)
    ]
    stretch = [
        [
            (
                facing[row][0] * turn[0][col]
                + facing[row][1] * turn[1][col]
                + facing[row][2] * turn[2][col]
            )
            * scales[col]
            for col in range(3)
        ]
        for row in range(2)
    ]
    cov_xx = (
        stretch[0][0] * stretch[0][0]
        + stretch[0][1] * stretch[0][1]
        + stretch[0][2] * stretch[0][2]
        + 0.3
    )
    cov_xy = (
        stretch[0][0] * stretch[1][0]
        + stretch[0][1] * stretch[1][1]
        + stretch[0][2] * stretch[1][2]
    )
    cov_yy = (
        stretch[1][0] * stretch[1][0]
        + stretch[1][1] * stretch[1][1]
        + stretch[1][2] * stretch[1][2]
        + 0.3
    )
    determinant = cov_xx * cov_yy - cov_xy * cov_xy
    safe = [placed[0], placed[1], depth]
    length = jnp.sqrt(safe[0] * safe[0] + safe[1] * safe[1] + safe[2] * safe[2])
    heading = [
        (rotation[0][col] * safe[0] + rotation[1][col] * safe[1] + rotation[2][col] * safe[2])
        / length
        for col in range(3)
    ]
    basis = harmonics(heading[0], heading[1], heading[2])
    colour = [
        0.5 + sum(basis[k] * params[11 + 3 * k + channel] for k in range(16)) for channel in range(3)
    ]
    log_opacity = -jnp.log1p(jnp.exp(-params[10]))
    return [
        screen_x,
        screen_y,
        cov_yy / determinant,
        -cov_xy / determinant,
        cov_xx / determinant,
        colour[0],
        colour[1],
        colour[2],
        log_opacity,
    ]


def similarity(mean_x, mean_y, power_x, power_y, cross):
    var_x = power_x - mean_x * mean_x
    var_y = power_y - mean_y * mean_y
    covar = cross - mean_x * mean_y
    upper = (2.0 * mean_x * mean_y + light_term) * (2.0 * covar + contrast_term)
    lower = (mean_x * mean_x + mean_y * mean_y + light_term) * (var_x + var_y + contrast_term)
    return upper / lower


def iota(shape, dim):
    return lax.broadcasted_iota(jnp.int32, shape, dim)


def split_three(values):
    high = values.astype(jnp.bfloat16)
    rest = values - high.astype(jnp.float32)
    middle = rest.astype(jnp.bfloat16)
    low = (rest - middle.astype(jnp.float32)).astype(jnp.bfloat16)
    return high, middle, low


def split_two(values):
    high = values.astype(jnp.bfloat16)
    return high, (values - high.astype(jnp.float32)).astype(jnp.bfloat16)


def one_hot(row, size, dtype=jnp.float32):
    hit = iota((size, row.shape[1]), 0) == row
    return jnp.where(hit, 1.0, 0.0).astype(dtype)


def pick_camera(view, camera_ref):
    picked = []
    for entry in range(12):
        value = jnp.full(view.shape, camera_ref[0, entry], jnp.float32)
        for number in range(1, VIEWS):
            value = jnp.where(view == float(number), camera_ref[number, entry], value)
        picked.append(value)
    return picked


def owner_kernel(
    geometry, offset, per_view, params_ref, camera_ref, index_ref, count_ref,
    message_ref, view_ref, low_ref, owner_ref
):
    strips = message_ref.shape[0]
    blocks = params_ref.shape[1]
    slots = index_ref.shape[1]
    span = slots // strips
    parts = span // LANES

    @pl.loop(0, strips)
    def _(strip):
        here = pl.ds(pl.multiple_of(strip * span, LANES), span)
        index = index_ref[:, here]
        low_ref[:, here] = one_hot(index & 127, LANES, jnp.bfloat16)
        view = (lax.rem(strip + offset, strips) // per_view).astype(jnp.float32)
        live = iota((1, span), 1) < count_ref[strip]
        mark = jnp.where(live, view, 0.0)
        owner_ref[:, here] = one_hot(index >> 7, blocks) * mark

    view = lax.dot_general(
        owner_ref[...].astype(jnp.bfloat16), low_ref[...], NT, preferred_element_type=jnp.float32
    )
    view_ref[...] = view
    camera = pick_camera(view, camera_ref)
    feet = project([params_ref[entry] for entry in range(59)], camera, *geometry)
    packed = jnp.concatenate(split_three(jnp.concatenate(feet, axis=0)), axis=1)

    @pl.loop(0, strips)
    def _(strip):
        here = pl.ds(pl.multiple_of(strip * span, LANES), span)
        low = low_ref[:, here]
        found = jnp.dot(
            packed, jnp.concatenate([low, low, low], axis=0), preferred_element_type=jnp.float32
        )
        high = one_hot(index_ref[:, here] >> 7, blocks)
        chosen = jnp.sum(found.reshape(FEET, blocks, span) * high[None], axis=1)
        for part in range(parts):
            message_ref[strip, part * FEET : (part + 1) * FEET, :] = chosen[
                :, part * LANES : (part + 1) * LANES
            ]
        message_ref[strip, parts * FEET : parts * FEET + 1, :] = jnp.full(
            (1, LANES), count_ref[strip].astype(jnp.float32)
        )


def source_hits(starts, ends, keys):
    return jnp.where((keys >= starts) & (keys < ends), 1.0, 0.0)


def blend_kernel(
    parts, tiles, chunk, arrived_ref, keys_ref, anchor_ref, powers_ref,
    rendered_ref, feet_ref, place_ref, alpha_ref, pass_ref, columns_ref, packed_ref
):
    strips, rows, _ = arrived_ref.shape
    total = keys_ref.shape[1]
    counts = arrived_ref[:, parts * FEET, :]
    order = iota((strips, strips), 0) >= iota((strips, strips), 1)
    ends = jnp.dot(
        jnp.where(order, 1.0, 0.0), counts, precision=exact_dot, preferred_element_type=jnp.float32
    )
    starts = ends - counts
    ends = ends[:, 0:1]
    starts = starts[:, 0:1]
    packed_ref[...] = jnp.concatenate(
        split_three(arrived_ref[...].reshape(strips * rows, LANES)), axis=1
    )
    powers = powers_ref[...]

    @pl.loop(0, total // chunk)
    def _(step):
        here = pl.ds(pl.multiple_of(step * chunk, LANES), chunk)
        keys = keys_ref[:, here].astype(jnp.float32)
        hits = source_hits(starts, ends, keys)
        slot = (keys - jnp.sum(hits * starts, axis=0, keepdims=True)).astype(jnp.int32)
        low = one_hot(slot & 127, LANES, jnp.bfloat16)
        found = jnp.dot(
            packed_ref[...],
            jnp.concatenate([low, low, low], axis=0),
            preferred_element_type=jnp.float32,
        )
        chosen = jnp.sum(found.reshape(strips, rows, chunk) * hits[:, None, :], axis=0)
        high = slot >> 7
        feet = chosen[0:FEET]
        for part in range(1, parts):
            feet = jnp.where(high == part, chosen[part * FEET : (part + 1) * FEET], feet)
        source = jnp.sum(hits * iota(hits.shape, 0).astype(jnp.float32), axis=0, keepdims=True)
        place_ref[0:1, here] = source.astype(jnp.int32)
        place_ref[1:2, here] = slot
        row = [feet[entry : entry + 1] for entry in range(FEET)]
        off_x = row[0] - anchor_ref[0:1, here]
        off_y = row[1] - anchor_ref[1:2, here]
        conic_a, conic_b, conic_c = row[2], row[3], row[4]
        feet_ref[:, here] = jnp.concatenate([off_x, off_y, conic_a, conic_b, conic_c], axis=0)
        terms = jnp.concatenate(
            [
                LOG2E
                * (
                    row[8]
                    - 0.5 * (conic_a * off_x * off_x + conic_c * off_y * off_y)
                    - conic_b * off_x * off_y
                ),
                LOG2E * (conic_a * off_x + conic_b * off_y),
                LOG2E * (conic_c * off_y + conic_b * off_x),
                (-0.5 * LOG2E) * conic_a,
                -LOG2E * conic_b,
                (-0.5 * LOG2E) * conic_c,
                jnp.zeros((2, chunk), jnp.float32),
            ],
            axis=0,
        )
        pieces = [piece.astype(jnp.float32) for piece in split_three(terms)]
        colours = jnp.concatenate(row[5:8] + [jnp.zeros((5, chunk), jnp.float32)], axis=0)
        columns = jnp.transpose(jnp.concatenate(pieces + [colours], axis=0))
        columns_ref[here, :] = columns
        power = jnp.dot(columns.astype(jnp.bfloat16), powers, preferred_element_type=jnp.float32)
        alpha_ref[here, :] = jnp.exp2(power)

    def forward(entry, carry):
        clear, red, green, blue = carry
        here = pl.ds(pl.multiple_of(entry * tiles, 8), tiles)
        pass_ref[here, :] = clear
        weight = alpha_ref[here, :] * clear
        tint = columns_ref[here, :]
        return (
            clear - weight,
            red + tint[:, 24:25] * weight,
            green + tint[:, 25:26] * weight,
            blue + tint[:, 26:27] * weight,
        )

    nothing = jnp.zeros((tiles, 256), jnp.float32)
    _, red, green, blue = lax.fori_loop(
        0, total // tiles, forward, (nothing + 1.0, nothing, nothing, nothing), unroll=2
    )
    rendered_ref[0] = red
    rendered_ref[1] = green
    rendered_ref[2] = blue


def loss_kernel(whole_ref, truth_ref, inside_ref, down_ref, back_ref, across_ref, grad_ref):
    rows = grad_ref.shape[1]
    centres = down_ref.shape[0]
    fields = []
    for channel in range(3):
        seen = whole_ref[channel]
        truth = truth_ref[channel]
        fields += [seen, truth, seen * seen, truth * truth, seen * truth]

    def smooth(matrix, items):
        stacked = jnp.concatenate(
            [
                jnp.dot(matrix, item, precision=exact_dot, preferred_element_type=jnp.float32)
                for item in items
            ],
            axis=0,
        )
        return jnp.dot(
            stacked, across_ref[...], precision=exact_dot, preferred_element_type=jnp.float32
        )

    smoothed = smooth(down_ref[...], fields)
    inside = inside_ref[...]
    partials = []
    for channel in range(3):
        mean_x, mean_y, power_x, power_y, cross = [
            smoothed[(5 * channel + item) * centres : (5 * channel + item + 1) * centres]
            for item in range(5)
        ]
        value, pull = jax.vjp(
            lambda first, second, third: similarity(first, mean_y, second, power_y, third),
            mean_x,
            power_x,
            cross,
        )
        partials += [
            jnp.where(inside > 0.0, part, 0.0) for part in pull(jnp.full_like(value, -1.0))
        ]
    spread = smooth(back_ref[...], partials)
    depth = 10
    for channel in range(3):
        first, second, third = [
            spread[(3 * channel + item) * rows : (3 * channel + item + 1) * rows]
            for item in range(3)
        ]
        seen = whole_ref[channel][depth : depth + rows]
        truth = truth_ref[channel][depth : depth + rows]
        grad_ref[channel] = first + 2.0 * seen * second + truth * third


def pull_kernel(
    parts, tiles, chunk, grad_ref, feet_ref, place_ref, alpha_ref, pass_ref, columns_ref,
    moments_ref, message_ref, change_ref, tints_ref
):
    total = feet_ref.shape[1]
    entries = total // tiles
    grads = [grad_ref[channel] for channel in range(3)]
    lane = iota((tiles, LANES), 1)

    def backward(step, behind):
        entry = entries - 1 - step
        here = pl.ds(pl.multiple_of(entry * tiles, 8), tiles)
        alpha = alpha_ref[here, :]
        clear = pass_ref[here, :]
        tint = columns_ref[here, :]
        shade = (
            grads[0] * tint[:, 24:25] + grads[1] * tint[:, 25:26] + grads[2] * tint[:, 26:27]
        )
        excess = shade - behind
        weight = alpha * clear
        change_ref[here, :] = weight * excess
        sums = [jnp.sum(weight * grad, axis=1, keepdims=True) for grad in grads]
        tints_ref[here, :] = jnp.where(
            lane == 0, sums[0], jnp.where(lane == 1, sums[1], jnp.where(lane == 2, sums[2], 0.0))
        )
        return behind + alpha * excess

    lax.fori_loop(
        0, entries, backward, jnp.zeros((tiles, 256), jnp.float32), unroll=2
    )
    message_ref[...] = jnp.zeros_like(message_ref)
    moments = moments_ref[...]
    return moments, total


def scatter_steps(strips, rows, parts, chunk, refs, moments, total):
    feet_ref, place_ref, message_ref, change_ref, tints_ref = refs

    @pl.loop(0, total // chunk)
    def _(step):
        here = pl.ds(pl.multiple_of(step * chunk, LANES), chunk)
        high, low = split_two(change_ref[here, :])
        sums = tints_ref[here, :] + jnp.dot(
            jnp.concatenate([high, low], axis=1), moments, preferred_element_type=jnp.float32
        )
        lines = jnp.transpose(sums)
        plain, by_x, by_y, by_xx, by_xy, by_yy = [lines[item : item + 1] for item in range(3, 9)]
        feet = feet_ref[:, here]
        off_x, off_y, conic_a, conic_b, conic_c = [feet[item : item + 1] for item in range(5)]
        far_x = by_x - off_x * plain
        far_y = by_y - off_y * plain
        far_xx = by_xx - 2.0 * off_x * by_x + off_x * off_x * plain
        far_yy = by_yy - 2.0 * off_y * by_y + off_y * off_y * plain
        far_xy = by_xy - off_x * by_y - off_y * by_x + off_x * off_y * plain
        slopes = jnp.concatenate(
            [
                conic_a * far_x + conic_b * far_y,
                conic_c * far_y + conic_b * far_x,
                -0.5 * far_xx,
                -far_xy,
                -0.5 * far_yy,
                lines[0:3],
                plain,
            ],
            axis=0,
        )
        source = place_ref[0:1, here]
        slot = place_ref[1:2, here]
        part_of = slot >> 7
        laid = [jnp.where(part_of == part, slopes, 0.0) for part in range(parts)]
        laid.append(jnp.zeros((rows - parts * FEET, chunk), jnp.float32))
        laid = jnp.concatenate(laid, axis=0)
        first = laid.astype(jnp.bfloat16).astype(jnp.float32)
        hits = one_hot(source, strips)[:, None, :]
        spread = jnp.concatenate(
            [
                (hits * piece[None]).reshape(strips * rows, chunk).astype(jnp.bfloat16)
                for piece in (first, laid - first)
            ],
            axis=1,
        )
        lows = one_hot(slot & 127, LANES, jnp.bfloat16)
        message_ref[...] += lax.dot_general(
            spread,
            jnp.concatenate([lows, lows], axis=1),
            NT,
            preferred_element_type=jnp.float32,
        )


def return_kernel(
    strips, rows, parts, tiles, chunk, grad_ref, feet_ref, place_ref, alpha_ref, pass_ref,
    columns_ref, moments_ref, message_ref, change_ref, tints_ref
):
    moments, total = pull_kernel(
        parts, tiles, chunk, grad_ref, feet_ref, place_ref, alpha_ref, pass_ref, columns_ref,
        moments_ref, message_ref, change_ref, tints_ref
    )
    refs = (feet_ref, place_ref, message_ref, change_ref, tints_ref)
    scatter_steps(strips, rows, parts, chunk, refs, moments, total)


def gather_kernel(
    geometry, params_ref, camera_ref, index_ref, view_ref, returned_ref, out_ref, sum_ref
):
    strips = returned_ref.shape[0]
    blocks = params_ref.shape[1]
    span = index_ref.shape[1] // strips
    parts = span // LANES
    sum_ref[...] = jnp.zeros_like(sum_ref)

    @pl.loop(0, strips)
    def _(strip):
        here = pl.ds(pl.multiple_of(strip * span, LANES), span)
        index = index_ref[:, here]
        low = one_hot(index & 127, LANES, jnp.bfloat16)
        high = one_hot(index >> 7, blocks)[None]
        block = returned_ref[strip]
        slopes = jnp.concatenate(
            [block[part * FEET : (part + 1) * FEET] for part in range(parts)], axis=1
        )
        first = slopes.astype(jnp.bfloat16).astype(jnp.float32)
        spread = jnp.concatenate(
            [
                (high * piece[:, None, :]).reshape(FEET * blocks, span).astype(jnp.bfloat16)
                for piece in (first, slopes - first)
            ],
            axis=1,
        )
        sum_ref[...] += lax.dot_general(
            spread, jnp.concatenate([low, low], axis=1), NT, preferred_element_type=jnp.float32
        )

    camera = pick_camera(view_ref[...], camera_ref)
    ignored, pull = jax.vjp(
        lambda values: project(values, camera, *geometry),
        [params_ref[entry] for entry in range(59)],
    )
    slopes = [sum_ref[entry * blocks : (entry + 1) * blocks, :] for entry in range(FEET)]
    for entry, slope in enumerate(pull(slopes)[0]):
        out_ref[entry] = slope


def window_weights():
    offsets = np.arange(11, dtype=np.float64) - 5.0
    raw = np.exp(-offsets * offsets / 4.5)
    return raw / raw.sum()


def band(out_rows, out_pad, in_pad, shift):
    weights = window_weights()
    matrix = np.zeros((out_pad, in_pad), np.float32)
    for row in range(out_rows):
        for tap in range(11):
            column = row + tap + shift
            if 0 <= column < in_pad:
                matrix[row, column] = weights[tap]
    return matrix


def pixel_powers():
    pixel = np.arange(256)
    along_x = pixel % 16 - 7.5
    along_y = pixel // 16 - 7.5
    return np.stack(
        [
            np.ones(256),
            along_x,
            along_y,
            along_x * along_x,
            along_x * along_y,
            along_y * along_y,
        ]
    )


def round_up(value, step):
    return -(-value // step) * step


def per_device(params, camera, send_index, send_count, tile_list, target):
    strips = lax.axis_size("strip")
    index = lax.axis_index("strip")
    per_view = strips // VIEWS
    offset = per_view // 2
    position = (index + offset) % strips
    rows_strip = target.shape[1]
    width = target.shape[2]
    view_rows = rows_strip * per_view
    focal = 0.5 * width
    geometry = (focal, 0.5 * width, 0.5 * view_rows)
    tiles, count = tile_list.shape
    total = tiles * count
    chunk = math.gcd(512, total)
    capacity = send_index.shape[1]
    parts = -(-capacity // LANES)
    span = parts * LANES
    rows = round_up(parts * FEET + 1, 16)
    local = params.shape[1]
    blocks = local // LANES
    vmem = pltpu.MemorySpace.VMEM
    smem = pltpu.MemorySpace.SMEM
    big = pltpu.CompilerParams(vmem_limit_bytes=56 * 1024 * 1024)

    def space(*kinds):
        return [pl.BlockSpec(memory_space=kind) for kind in kinds]

    def shaped(*shape, dtype=jnp.float32):
        return jax.ShapeDtypeStruct(shape, dtype)

    params_cut = params.reshape(59, blocks, LANES)
    slot_index = jnp.pad(send_index, ((0, 0), (0, span - capacity))).reshape(1, strips * span)
    message, view = pl.pallas_call(
        functools.partial(owner_kernel, geometry, offset, per_view),
        out_shape=(shaped(strips, rows, LANES), shaped(blocks, LANES)),
        in_specs=space(vmem, smem, vmem, smem),
        out_specs=tuple(space(vmem, vmem)),
        scratch_shapes=[
            pltpu.VMEM((LANES, strips * span), jnp.bfloat16),
            pltpu.VMEM((blocks, strips * span), jnp.float32),
        ],
        compiler_params=big,
        name="owner_project",
    )(params_cut, camera, slot_index, send_count)
    arrived = lax.all_to_all(message, "strip", split_axis=0, concat_axis=0, tiled=True)

    keys = tile_list.T.reshape(1, total)
    tile_cols = width // 16
    tile_num = jnp.arange(tiles, dtype=jnp.int32)
    anchor_x = tile_num % tile_cols * 16 + 8
    anchor_y = (position % per_view * (rows_strip // 16) + tile_num // tile_cols) * 16 + 8
    anchor = jnp.tile(jnp.stack([anchor_x, anchor_y]).astype(jnp.float32), (1, count))
    monomials = pixel_powers()
    powers = np.zeros((32, 256), np.float32)
    for piece in range(3):
        powers[8 * piece : 8 * piece + 6] = monomials
    moments = np.zeros((512, LANES), np.float32)
    moments[0:256, 3:9] = monomials.T
    moments[256:512, 3:9] = monomials.T
    rendered, feet, place, alpha, clear, columns = pl.pallas_call(
        functools.partial(blend_kernel, parts, tiles, chunk),
        out_shape=(
            shaped(3, tiles, 256),
            shaped(5, total),
            shaped(2, total, dtype=jnp.int32),
            shaped(total, 256),
            shaped(total, 256),
            shaped(total, 32),
        ),
        in_specs=space(vmem, vmem, vmem, vmem),
        out_specs=tuple(space(vmem, vmem, vmem, vmem, vmem, vmem)),
        scratch_shapes=[pltpu.VMEM((strips * rows, 3 * LANES), jnp.bfloat16)],
        compiler_params=big,
        name="blend",
    )(arrived, keys, anchor, jnp.asarray(powers, jnp.bfloat16))

    depth = 10
    high_rows = round_up(rows_strip + 2 * depth, 8)
    centres = round_up(rows_strip + depth, 8)
    step = position % per_view
    top = step != 0
    bottom = step != per_view - 1
    ahead = [(i, (i + 1) % strips) for i in range(strips)]
    behind = [((i + 1) % strips, i) for i in range(strips)]

    def with_halo(image):
        above = lax.ppermute(image[:, rows_strip - depth :, :], "strip", ahead)
        below = lax.ppermute(image[:, :depth, :], "strip", behind)
        fill = jnp.zeros((3, high_rows - rows_strip - 2 * depth, width), jnp.float32)
        return jnp.concatenate(
            [jnp.where(top, above, 0.0), image, jnp.where(bottom, below, 0.0), fill], axis=1
        )

    strip_rows = rows_strip // 16
    image = rendered.reshape(3, strip_rows, tile_cols, 16, 16)
    image = image.transpose(0, 1, 3, 2, 4).reshape(3, rows_strip, width)
    centre = jnp.arange(centres, dtype=jnp.int32)[:, None]
    inside = ((centre >= 5) | top) & ((centre < rows_strip + 5) | bottom)
    inside = (inside & (centre < rows_strip + depth)).astype(jnp.float32)
    render_grad = pl.pallas_call(
        loss_kernel,
        out_shape=shaped(3, rows_strip, width),
        compiler_params=big,
        name="window_loss",
    )(
        with_halo(image),
        with_halo(target),
        inside,
        band(rows_strip + depth, centres, high_rows, 0),
        band(rows_strip, rows_strip, centres, 0),
        band(width, width, width, -5),
    )
    cotangent = render_grad.reshape(3, strip_rows, 16, tile_cols, 16)
    cotangent = cotangent.transpose(0, 1, 3, 2, 4).reshape(3, tiles, 256)
    slopes = pl.pallas_call(
        functools.partial(return_kernel, strips, rows, parts, tiles, chunk),
        out_shape=shaped(strips * rows, LANES),
        scratch_shapes=[
            pltpu.VMEM((total, 256), jnp.float32),
            pltpu.VMEM((total, LANES), jnp.float32),
        ],
        compiler_params=big,
        name="blend_pull",
    )(cotangent, feet, place, alpha, clear, columns, jnp.asarray(moments, jnp.bfloat16))
    returned = lax.all_to_all(
        slopes.reshape(strips, rows, LANES), "strip", split_axis=0, concat_axis=0, tiled=True
    )
    grads = pl.pallas_call(
        functools.partial(gather_kernel, geometry),
        out_shape=shaped(59, blocks, LANES),
        in_specs=space(vmem, smem, vmem, vmem, vmem),
        scratch_shapes=[pltpu.VMEM((FEET * blocks, LANES), jnp.float32)],
        compiler_params=big,
        name="owner_pull",
    )(params_cut, camera, slot_index, view, returned)
    return grads.reshape(59, local)


def solution(mesh):
    return jax.shard_map(
        per_device,
        mesh=mesh,
        in_specs=(
            P(None, "strip"),
            P(),
            P("strip", None),
            P("strip"),
            P("strip", None),
            P(None, "strip", None),
        ),
        out_specs=P(None, "strip"),
        check_vma=False,
    )
```

profile of v0, /device:TPU:0, one launch (start us, length us, event | category | flops | bytes accessed | tf_op | source)
XLA Modules:
  0.0 160.7 jit_solution(11577459867544511199)
XLA Ops:
  0.0 1.5 copy.26
  1.6 0.0 copy-start.2
  1.6 1.1 slice.18.params_ref
  2.7 0.0 copy-done.2
  2.7 0.0 copy-start.1
  2.7 0.7 copy.27
  3.3 0.0 copy-start.3
  3.4 16.4 %owner_project.1 = (f32[32,32,128]{2,1,0:T(8,128)}, f32[40,128]{1,0:T(8,128)}) custom-call(f32[59,40,128]{2,1,0:T(8,128)} %slice.18.params_ref, f32[4,12]{1,0:T(4,128)} %camera_ref.3, s32[1,12288]{1,0:T(1,128)} %bitcast.28, s32[32]{0:T(128)} %count_ref.1), custom_call_target="tpu_custom_call" | custom-call | tf_op jit(solution)/shard_map/owner_project/pallas_call | solution.py:610
  19.8 7.3 %all-to-all-start = ((f32[32,32,128]{2,1,0:T(8,128)}), f32[32,32,128]{2,1,0:T(8,128)S(1)}, u32[]{:S(2)}, u32[]{:S(2)}) async-start(f32[32,32,128]{2,1,0:T(8,128)} %get-tuple-element.14), calls=%async_computation | async-start | bytes 1048576 | tf_op jit(solution)/shard_map/all_to_all | solution.py:622
  27.1 0.0 copy-done.1
  27.1 5.3 %collective-permute-start.3 = (f32[3,10,640]{2,1,0:T(8,128)S(1)}, f32[3,10,640]{2,1,0:T(8,128)S(1)}, u32[]{:S(2)}, u32[]{:S(2)}) collective-permute-start(f32[3,10,640]{2,1,0:T(8,128)S(1)} %get-tuple-element.22), channel_id=1, source_target_pairs={{1,0},{2,1},{3,2},{4,3},{5,4},{6,5},{7,6},{8,7},{9,8},{10,9},{11,1... | collective-permute-start | bytes 230408 | tf_op jit(solution)/shard_map/ppermute | solution.py:665
  32.4 0.0 collective-permute-start.2
  32.4 0.8 tile.10.anchor_ref
  33.2 0.0 copy-done.3
  33.2 0.1 copy.20
  33.3 0.7 reshape.139.keys_ref
  34.0 0.1 pad.12.clone
  34.1 0.6 fusion.3.inside_ref
  34.7 2.9 %collective-permute-done.3 = f32[3,10,640]{2,1,0:T(8,128)S(1)} collective-permute-done((f32[3,10,640]{2,1,0:T(8,128)S(1)}, f32[3,10,640]{2,1,0:T(8,128)S(1)}, u32[]{:S(2)}, u32[]{:S(2)}) %collective-permute-start.3) | collective-permute-done | bytes 76832 | tf_op jit(solution)/shard_map/ppermute | solution.py:665
  37.6 6.4 %all-to-all-done.arrived_ref = f32[32,32,128]{2,1,0:T(8,128)S(1)} async-done(((f32[32,32,128]{2,1,0:T(8,128)}), f32[32,32,128]{2,1,0:T(8,128)S(1)}, u32[]{:S(2)}, u32[]{:S(2)}) %all-to-all-start) | async-done | bytes 524320 | tf_op jit(solution)/shard_map/all_to_all | solution.py:622
  43.9 0.0 copy-start
  43.9 0.8 copy-done
  44.7 24.6 %blend.1 = (f32[3,40,256]{2,1,0:T(8,128)}, f32[5,5120]{1,0:T(8,128)}, s32[2,5120]{1,0:T(2,128)}, f32[5120,256]{1,0:T(8,128)}, f32[5120,256]{1,0:T(8,128)}, /*index=5*/f32[5120,32]{1,0:T(8,128)}) custom-call(f32[32,32,128]{2,1,0:T(8,128)} %copy-done, s32[1,5120]{1,0:T(1,128)} %reshape.139.keys_ref, f32[2,5120]{1,0:T(2,128)} %tile.10.anchor_ref, ...), custom_call_target="tpu_custom_call" | custom-call | tf_op jit(solution)/shard_map/blend/pallas_call | solution.py:637
  69.3 1.1 copy.21
  70.4 0.3 copy.22
  70.7 0.3 reshape.141
  71.1 0.1 collective-permute-start
  71.1 0.0 collective-permute-done.2
  71.2 5.5 %collective-permute-start.1 = (f32[3,10,640]{2,1,0:T(8,128)S(1)}, f32[3,10,640]{2,1,0:T(8,128)S(1)}, u32[]{:S(2)}, u32[]{:S(2)}) collective-permute-start(f32[3,10,640]{2,1,0:T(8,128)S(1)} %get-tuple-element.24), channel_id=1, source_target_pairs={{1,0},{2,1},{3,2},{4,3},{5,4},{6,5},{7,6},{8,7},{9,8},{10,9},{11,1... | collective-permute-start | bytes 230408 | tf_op jit(solution)/shard_map/ppermute | solution.py:665
  76.7 2.4 %collective-permute-done = f32[3,10,640]{2,1,0:T(8,128)S(1)} collective-permute-done((f32[3,10,640]{2,1,0:T(8,128)S(1)}, f32[3,10,640]{2,1,0:T(8,128)S(1)}, u32[]{:S(2)}, u32[]{:S(2)}) %collective-permute-start) | collective-permute-done | bytes 76832 | tf_op jit(solution)/shard_map/ppermute | solution.py:664
  79.1 0.0 collective-permute-done.1
  79.2 0.9 maximum_maximum_fusion.1
  80.1 9.9 %window_loss.1 = f32[3,16,640]{2,1,0:T(8,128)} custom-call(f32[3,40,640]{2,1,0:T(8,128)} %get-tuple-element.26.whole_ref, f32[3,40,640]{2,1,0:T(8,128)} %get-tuple-element.25.truth_ref, f32[32,1]{1,0:T(8,128)} %fusion.3.inside_ref, f32[32,40]{1,0:T(8,128)} %constant.76.clone.down_ref, f32[16,32]{1,0:T(8,128)} %constant.77.clone.back_ref, ...), custom_call_target="tpu_custom_call" | custom-call | tf_op jit(solution)/shard_map/window_loss/pallas_call | solution.py:677
  90.0 1.2 reshape.142
  91.3 0.3 copy.24
  91.6 0.8 copy.25.grad_ref
  92.4 30.6 %blend_pull.1 = f32[1024,128]{1,0:T(8,128)} custom-call(f32[3,40,256]{2,1,0:T(8,128)} %copy.25.grad_ref, f32[5,5120]{1,0:T(8,128)} %get-tuple-element.16.feet_ref, s32[2,5120]{1,0:T(2,128)} %get-tuple-element.17.place_ref, f32[5120,256]{1,0:T(8,128)} %get-tuple-element.18.alpha_ref, f32[5120,256]{1,0:T(8,128)} %get-tuple-element.19.pass_ref, ...), custom_call_target="tpu_custom_call" | custom-call | tf_op jit(solution)/shard_map/blend_pull/pallas_call | solution.py:692
  123.0 21.5 %all_to_all.10.returned_ref = f32[32,32,128]{2,1,0:T(8,128)} all-to-all(f32[32,32,128]{2,1,0:T(8,128)} %bitcast.24), channel_id=1, replica_groups=mesh['strip'=32] {'strip'}, dimensions={0} | all-to-all | bytes 1048576 | tf_op jit(solution)/shard_map/all_to_all | solution.py:702
  144.4 13.6 %owner_pull.1 = f32[59,40,128]{2,1,0:T(8,128)} custom-call(f32[59,40,128]{2,1,0:T(8,128)} %slice.18.params_ref, f32[4,12]{1,0:T(4,128)} %camera_ref.3, s32[1,12288]{1,0:T(1,128)} %bitcast.29, f32[40,128]{1,0:T(8,128)} %get-tuple-element.13.view_ref, f32[32,32,128]{2,1,0:T(8,128)} %all_to_all.10.returned_ref), custom_call_target="tpu_custom_call" | custom-call | tf_op jit(solution)/shard_map/owner_pull/pallas_call | solution.py:705
  158.0 1.4 pad.15
  159.4 1.3 copy.28
  (11 shorter events, 0.1 us)
Async XLA Ops:
  1.6 1.1 copy-start.2
  2.7 24.4 %copy-start.1 = (f32[3,16,640]{2,1,0:T(8,128)S(1)}, f32[3,16,640]{2,1,0:T(8,128)}, u32[]{:S(2)}) copy-start(f32[3,16,640]{2,1,0:T(8,128)} %param.16) | copy-start | bytes 368644
  3.3 29.8 %copy-start.3 = (s32[40,128]{1,0:T(8,128)S(1)}, s32[40,128]{1,0:T(8,128)}, u32[]{:S(2)}) copy-start(s32[40,128]{1,0:T(8,128)} %param.15) | copy-start | bytes 61444
  19.8 24.2 %all-to-all-start = ((f32[32,32,128]{2,1,0:T(8,128)}), f32[32,32,128]{2,1,0:T(8,128)S(1)}, u32[]{:S(2)}, u32[]{:S(2)}) async-start(f32[32,32,128]{2,1,0:T(8,128)} %get-tuple-element.14), calls=%async_computation | async-start | bytes 1048576 | tf_op jit(solution)/shard_map/all_to_all | solution.py:622
  27.1 10.4 %collective-permute-start.3 = (f32[3,10,640]{2,1,0:T(8,128)S(1)}, f32[3,10,640]{2,1,0:T(8,128)S(1)}, u32[]{:S(2)}, u32[]{:S(2)}) collective-permute-start(f32[3,10,640]{2,1,0:T(8,128)S(1)} %get-tuple-element.22), channel_id=1, source_target_pairs={{1,0},{2,1},{3,2},{4,3},{5,4},{6,5},{7,6},{8,7},{9,8},{10,9},{11,1... | collective-permute-start | bytes 230408 | tf_op jit(solution)/shard_map/ppermute | solution.py:665
  32.4 38.7 %collective-permute-start.2 = (f32[3,10,640]{2,1,0:T(8,128)S(1)}, f32[3,10,640]{2,1,0:T(8,128)S(1)}, u32[]{:S(2)}, u32[]{:S(2)}) collective-permute-start(f32[3,10,640]{2,1,0:T(8,128)S(1)} %get-tuple-element.21), channel_id=1, source_target_pairs={{0,1},{1,2},{2,3},{3,4},{4,5},{5,6},{6,7},{7,8},{8,9},{9,10},{10,1... | collective-permute-start | bytes 230408 | tf_op jit(solution)/shard_map/ppermute | solution.py:664
  43.9 0.8 copy-start
  71.1 8.1 %collective-permute-start = (f32[3,10,640]{2,1,0:T(8,128)S(1)}, f32[3,10,640]{2,1,0:T(8,128)S(1)}, u32[]{:S(2)}, u32[]{:S(2)}) collective-permute-start(f32[3,10,640]{2,1,0:T(8,128)S(1)} %get-tuple-element.23), channel_id=1, source_target_pairs={{0,1},{1,2},{2,3},{3,4},{4,5},{5,6},{6,7},{7,8},{8,9},{9,10},{10,1... | collective-permute-start | bytes 230408 | tf_op jit(solution)/shard_map/ppermute | solution.py:664
  71.2 8.0 %collective-permute-start.1 = (f32[3,10,640]{2,1,0:T(8,128)S(1)}, f32[3,10,640]{2,1,0:T(8,128)S(1)}, u32[]{:S(2)}, u32[]{:S(2)}) collective-permute-start(f32[3,10,640]{2,1,0:T(8,128)S(1)} %get-tuple-element.24), channel_id=1, source_target_pairs={{1,0},{2,1},{3,2},{4,3},{5,4},{6,5},{7,6},{8,7},{9,8},{10,9},{11,1... | collective-permute-start | bytes 230408 | tf_op jit(solution)/shard_map/ppermute | solution.py:665
where the time goes:
time: 161 us
  Pallas kernels  95.1 us (59%)
  blocking collectives  21.5 us (13%)
  starting transfers between devices  18.2 us (11%)
  local copies, waits for them, and re-layouts  12.5 us (8%)
  waiting for transfers between devices  11.7 us (7%)
  other arithmetic  1.61 us (1%)
    pallas_call x1, Pallas kernels, per_device(): pl.pallas_call(functools.partial(return_kernel, strips, rows, parts, tile...  30.6 us
    pallas_call x1, Pallas kernels, per_device(): pl.pallas_call(functools.partial(blend_kernel, parts, tiles, chunk), out_...  24.6 us
    all_to_all x1, blocking collectives, per_device(): lax.all_to_all(slopes.reshape(strips, rows, LANES), 'strip', split_axis=0...  21.5 us
    pallas_call x1, Pallas kernels, per_device(): pl.pallas_call(functools.partial(owner_kernel, geometry, offset, per_view...  16.4 us
    pallas_call x1, Pallas kernels, per_device(): pl.pallas_call(functools.partial(gather_kernel, geometry), out_shape=shap...  13.6 us
    ppermute x2, starting transfers between devices, with_halo(): below = lax.ppermute(image[:, :depth, :], 'strip', behind)  10.8 us
    pallas_call x1, Pallas kernels, per_device(): pl.pallas_call(loss_kernel, out_shape=shaped(3, rows_strip, width), compi...  9.95 us
    all_to_all x1, starting transfers between devices, per_device(): lax.all_to_all(message, 'strip', split_axis=0, concat_axis=0, tiled=True)  7.3 us
  transfers between devices with their start and end apart: 5, of which 3 were waited for; matrix products, arithmetic and copies ran while one was open for 3% of the time, Pallas kernels for 15%

commit v1 on v0

--- a/solution.py
+++ b/solution.py
@@ -231,17 +231,21 @@
     view_ref[...] = view
     camera = pick_camera(view, camera_ref)
     feet = project([params_ref[entry] for entry in range(59)], camera, *geometry)
-    packed = jnp.concatenate(split_three(jnp.concatenate(feet, axis=0)), axis=1)
+    high, middle, third = split_three(jnp.concatenate(feet, axis=0))
+    packed = jnp.concatenate([high, middle], axis=1)
+    third = third[0 : 2 * blocks]
 
     @pl.loop(0, strips)
     def _(strip):
         here = pl.ds(pl.multiple_of(strip * span, LANES), span)
         low = low_ref[:, here]
         found = jnp.dot(
-            packed, jnp.concatenate([low, low, low], axis=0), preferred_element_type=jnp.float32
-        )
+            packed, jnp.concatenate([low, low], axis=0), preferred_element_type=jnp.float32
+        ).reshape(FEET, blocks, span)
+        fine = jnp.dot(third, low, preferred_element_type=jnp.float32).reshape(2, blocks, span)
+        found = jnp.concatenate([found[0:2] + fine, found[2:]], axis=0)
         high = one_hot(index_ref[:, here] >> 7, blocks)
-        chosen = jnp.sum(found.reshape(FEET, blocks, span) * high[None], axis=1)
+        chosen = jnp.sum(found * high[None], axis=1)
         for part in range(parts):
             message_ref[strip, part * FEET : (part + 1) * FEET, :] = chosen[
                 :, part * LANES : (part + 1) * LANES
@@ -257,7 +261,7 @@
 
 def blend_kernel(
     parts, tiles, chunk, arrived_ref, keys_ref, anchor_ref, powers_ref,
-    rendered_ref, feet_ref, place_ref, alpha_ref, pass_ref, columns_ref, packed_ref
+    rendered_ref, feet_ref, place_ref, columns_ref, alpha_ref, packed_ref, third_ref
 ):
     strips, rows, _ = arrived_ref.shape
     total = keys_ref.shape[1]
@@ -269,9 +273,17 @@
     starts = ends - counts
     ends = ends[:, 0:1]
     starts = starts[:, 0:1]
-    packed_ref[...] = jnp.concatenate(
-        split_three(arrived_ref[...].reshape(strips * rows, LANES)), axis=1
-    )
+    span = parts * LANES
+    for foot in range(FEET):
+        block = jnp.concatenate(
+            [arrived_ref[:, part * FEET + foot, :] for part in range(parts)], axis=1
+        )
+        high, middle, third = split_three(block)
+        here = slice(foot * strips, (foot + 1) * strips)
+        packed_ref[here, 0:span] = high
+        packed_ref[here, span : 2 * span] = middle
+        if foot < 2:
+            third_ref[here, :] = third
     powers = powers_ref[...]
 
     @pl.loop(0, total // chunk)
@@ -280,17 +292,17 @@
         keys = keys_ref[:, here].astype(jnp.float32)
         hits = source_hits(starts, ends, keys)
         slot = (keys - jnp.sum(hits * starts, axis=0, keepdims=True)).astype(jnp.int32)
-        low = one_hot(slot & 127, LANES, jnp.bfloat16)
+        low = one_hot(slot, span, jnp.bfloat16)
         found = jnp.dot(
             packed_ref[...],
-            jnp.concatenate([low, low, low], axis=0),
+            jnp.concatenate([low, low], axis=0),
             preferred_element_type=jnp.float32,
-        )
-        chosen = jnp.sum(found.reshape(strips, rows, chunk) * hits[:, None, :], axis=0)
-        high = slot >> 7
-        feet = chosen[0:FEET]
-        for part in range(1, parts):
-            feet = jnp.where(high == part, chosen[part * FEET : (part + 1) * FEET], feet)
+        ).reshape(FEET, strips, chunk)
+        fine = jnp.dot(
+            third_ref[...], low, preferred_element_type=jnp.float32
+        ).reshape(2, strips, chunk)
+        found = jnp.concatenate([found[0:2] + fine, found[2:]], axis=0)
+        feet = jnp.sum(found * hits[None], axis=1)
         source = jnp.sum(hits * iota(hits.shape, 0).astype(jnp.float32), axis=0, keepdims=True)
         place_ref[0:1, here] = source.astype(jnp.int32)
         place_ref[1:2, here] = slot
@@ -326,7 +338,6 @@
     def forward(entry, carry):
         clear, red, green, blue = carry
         here = pl.ds(pl.multiple_of(entry * tiles, 8), tiles)
-        pass_ref[here, :] = clear
         weight = alpha_ref[here, :] * clear
         tint = columns_ref[here, :]
         return (
@@ -396,12 +407,31 @@
 
 
 def pull_kernel(
-    parts, tiles, chunk, grad_ref, feet_ref, place_ref, alpha_ref, pass_ref, columns_ref,
-    moments_ref, message_ref, change_ref, tints_ref
+    parts, tiles, chunk, grad_ref, feet_ref, place_ref, columns_ref, powers_ref,
+    moments_ref, change_ref, tints_ref, alpha_ref, pass_ref
 ):
     total = feet_ref.shape[1]
     entries = total // tiles
     grads = [grad_ref[channel] for channel in range(3)]
+    powers = powers_ref[...]
+
+    @pl.loop(0, total // chunk)
+    def _(step):
+        here = pl.ds(pl.multiple_of(step * chunk, LANES), chunk)
+        alpha_ref[here, :] = jnp.exp2(
+            jnp.dot(
+                columns_ref[here, :].astype(jnp.bfloat16),
+                powers,
+                preferred_element_type=jnp.float32,
+            )
+        )
+
+    def forward(entry, clear):
+        here = pl.ds(pl.multiple_of(entry * tiles, 8), tiles)
+        pass_ref[here, :] = clear
+        return clear - alpha_ref[here, :] * clear
+
+    lax.fori_loop(0, entries, forward, jnp.ones((tiles, 256), jnp.float32), unroll=4)
     lane = iota((tiles, LANES), 1)
 
     def backward(step, behind):
@@ -425,13 +455,13 @@
     lax.fori_loop(
         0, entries, backward, jnp.zeros((tiles, 256), jnp.float32), unroll=2
     )
-    message_ref[...] = jnp.zeros_like(message_ref)
     moments = moments_ref[...]
     return moments, total
 
 
 def scatter_steps(strips, rows, parts, chunk, refs, moments, total):
-    feet_ref, place_ref, message_ref, change_ref, tints_ref = refs
+    feet_ref, place_ref, message_ref, change_ref, tints_ref, sum_ref = refs
+    sum_ref[...] = jnp.zeros_like(sum_ref)
 
     @pl.loop(0, total // chunk)
     def _(step):
@@ -463,37 +493,39 @@
         )
         source = place_ref[0:1, here]
         slot = place_ref[1:2, here]
-        part_of = slot >> 7
-        laid = [jnp.where(part_of == part, slopes, 0.0) for part in range(parts)]
-        laid.append(jnp.zeros((rows - parts * FEET, chunk), jnp.float32))
-        laid = jnp.concatenate(laid, axis=0)
-        first = laid.astype(jnp.bfloat16).astype(jnp.float32)
-        hits = one_hot(source, strips)[:, None, :]
+        first = slopes.astype(jnp.bfloat16).astype(jnp.float32)
+        hits = one_hot(source, strips)[None]
         spread = jnp.concatenate(
             [
-                (hits * piece[None]).reshape(strips * rows, chunk).astype(jnp.bfloat16)
-                for piece in (first, laid - first)
+                (hits * piece[:, None, :]).reshape(FEET * strips, chunk).astype(jnp.bfloat16)
+                for piece in (first, slopes - first)
             ],
             axis=1,
         )
-        lows = one_hot(slot & 127, LANES, jnp.bfloat16)
-        message_ref[...] += lax.dot_general(
+        lows = one_hot(slot, parts * LANES, jnp.bfloat16)
+        sum_ref[...] += lax.dot_general(
             spread,
             jnp.concatenate([lows, lows], axis=1),
             NT,
             preferred_element_type=jnp.float32,
         )
 
+    for foot in range(FEET):
+        for part in range(parts):
+            message_ref[:, part * FEET + foot, :] = sum_ref[
+                foot * strips : (foot + 1) * strips, part * LANES : (part + 1) * LANES
+            ]
+
 
 def return_kernel(
-    strips, rows, parts, tiles, chunk, grad_ref, feet_ref, place_ref, alpha_ref, pass_ref,
-    columns_ref, moments_ref, message_ref, change_ref, tints_ref
+    strips, rows, parts, tiles, chunk, grad_ref, feet_ref, place_ref, columns_ref, powers_ref,
+    moments_ref, message_ref, change_ref, tints_ref, sum_ref, alpha_ref, pass_ref
 ):
     moments, total = pull_kernel(
-        parts, tiles, chunk, grad_ref, feet_ref, place_ref, alpha_ref, pass_ref, columns_ref,
-        moments_ref, message_ref, change_ref, tints_ref
-    )
-    refs = (feet_ref, place_ref, message_ref, change_ref, tints_ref)
+        parts, tiles, chunk, grad_ref, feet_ref, place_ref, columns_ref, powers_ref,
+        moments_ref, change_ref, tints_ref, alpha_ref, pass_ref
+    )
+    refs = (feet_ref, place_ref, message_ref, change_ref, tints_ref, sum_ref)
     scatter_steps(strips, rows, parts, chunk, refs, moments, total)
 
 
@@ -634,19 +666,21 @@
     moments = np.zeros((512, LANES), np.float32)
     moments[0:256, 3:9] = monomials.T
     moments[256:512, 3:9] = monomials.T
-    rendered, feet, place, alpha, clear, columns = pl.pallas_call(
+    rendered, feet, place, columns = pl.pallas_call(
         functools.partial(blend_kernel, parts, tiles, chunk),
         out_shape=(
             shaped(3, tiles, 256),
             shaped(5, total),
             shaped(2, total, dtype=jnp.int32),
-            shaped(total, 256),
-            shaped(total, 256),
             shaped(total, 32),
         ),
         in_specs=space(vmem, vmem, vmem, vmem),
-        out_specs=tuple(space(vmem, vmem, vmem, vmem, vmem, vmem)),
-        scratch_shapes=[pltpu.VMEM((strips * rows, 3 * LANES), jnp.bfloat16)],
+        out_specs=tuple(space(vmem, vmem, vmem, vmem)),
+        scratch_shapes=[
+            pltpu.VMEM((total, 256), jnp.float32),
+            pltpu.VMEM((FEET * strips, 2 * span), jnp.bfloat16),
+            pltpu.VMEM((2 * strips, span), jnp.bfloat16),
+        ],
         compiler_params=big,
         name="blend",
     )(arrived, keys, anchor, jnp.asarray(powers, jnp.bfloat16))
@@ -691,16 +725,26 @@
     cotangent = cotangent.transpose(0, 1, 3, 2, 4).reshape(3, tiles, 256)
     slopes = pl.pallas_call(
         functools.partial(return_kernel, strips, rows, parts, tiles, chunk),
-        out_shape=shaped(strips * rows, LANES),
+        out_shape=shaped(strips, rows, LANES),
         scratch_shapes=[
             pltpu.VMEM((total, 256), jnp.float32),
             pltpu.VMEM((total, LANES), jnp.float32),
+            pltpu.VMEM((FEET * strips, span), jnp.float32),
+            pltpu.VMEM((total, 256), jnp.float32),
+            pltpu.VMEM((total, 256), jnp.float32),
         ],
         compiler_params=big,
         name="blend_pull",
-    )(cotangent, feet, place, alpha, clear, columns, jnp.asarray(moments, jnp.bfloat16))
+    )(
+        cotangent,
+        feet,
+        place,
+        columns,
+        jnp.asarray(powers, jnp.bfloat16),
+        jnp.asarray(moments, jnp.bfloat16),
+    )
     returned = lax.all_to_all(
-        slopes.reshape(strips, rows, LANES), "strip", split_axis=0, concat_axis=0, tiled=True
+        slopes, "strip", split_axis=0, concat_axis=0, tiled=True
     )
     grads = pl.pallas_call(
         functools.partial(gather_kernel, geometry),

time: 161 us -> 151 us (0.938)
  Pallas kernels: 95.1 us -> 84.8 us
    pallas_call x1, Pallas kernels: 24.6 us -> 18.5 us  [per_device(): pl.pallas_call(functools.partial(blend_kernel, parts, tiles, chunk), out_...]
    pallas_call x1, Pallas kernels: 16.4 us -> 14.2 us  [per_device(): pl.pallas_call(functools.partial(owner_kernel, geometry, offset, per_view...]
    pallas_call x1, Pallas kernels: 30.6 us -> 28.6 us  [per_device(): pl.pallas_call(functools.partial(return_kernel, strips, rows, parts, tile...]
  transfers between devices with their start and end apart: 5 -> 5, of which waited for: 3 -> 3; matrix products, arithmetic and copies ran while one was open for 3% -> 3% of each run, Pallas kernels for 15% -> 12%
where the time goes in v1:
time: 151 us; the launch traced here: 150 us
  Pallas kernels  84.8 us (56%)
  blocking collectives  21.5 us (14%)
  starting transfers between devices  18.2 us (12%)
  local copies, waits for them, and re-layouts  12.5 us (8%)
  waiting for transfers between devices  11.7 us (8%)
  other arithmetic  1.62 us (1%)
    pallas_call x1, Pallas kernels, per_device(): pl.pallas_call(functools.partial(return_kernel, strips, rows, parts, tile...  28.6 us
    all_to_all x1, blocking collectives, per_device(): lax.all_to_all(slopes, 'strip', split_axis=0, concat_axis=0, tiled=True)  21.5 us
    pallas_call x1, Pallas kernels, per_device(): pl.pallas_call(functools.partial(blend_kernel, parts, tiles, chunk), out_...  18.5 us
    pallas_call x1, Pallas kernels, per_device(): pl.pallas_call(functools.partial(owner_kernel, geometry, offset, per_view...  14.2 us
    pallas_call x1, Pallas kernels, per_device(): pl.pallas_call(functools.partial(gather_kernel, geometry), out_shape=shap...  13.7 us
    ppermute x2, starting transfers between devices, with_halo(): below = lax.ppermute(image[:, :depth, :], 'strip', behind)  10.8 us
    pallas_call x1, Pallas kernels, per_device(): pl.pallas_call(loss_kernel, out_shape=shaped(3, rows_strip, width), compi...  9.93 us
    all_to_all x1, starting transfers between devices, per_device(): lax.all_to_all(message, 'strip', split_axis=0, concat_axis=0, tiled=True)  7.3 us
  transfers between devices with their start and end apart: 5, of which 3 were waited for; matrix products, arithmetic and copies ran while one was open for 3% of the time, Pallas kernels for 12%

profile of v1, /device:TPU:0, one launch (start us, length us, event | category | flops | bytes accessed | tf_op | source)
XLA Modules:
  0.0 150.5 jit_solution(14098452052266442597)
XLA Ops:
  0.0 1.5 %copy.27 = f32[8,8,40,128]{3,2,1,0:T(8,128)S(1)} copy(f32[8,8,40,128]{3,1,2,0:T(8,128)} %bitcast.25) | data formatting | bytes 2621440
  1.6 0.0 copy-start.2
  1.6 1.1 slice.18.params_ref
  2.7 0.0 copy-done.2
  2.7 0.0 copy-start.1
  2.7 0.7 copy.28
  3.3 0.0 copy-start.3
  3.4 14.2 %owner_project.1 = (f32[32,32,128]{2,1,0:T(8,128)}, f32[40,128]{1,0:T(8,128)}) custom-call(f32[59,40,128]{2,1,0:T(8,128)} %slice.18.params_ref, f32[4,12]{1,0:T(4,128)} %camera_ref.3, s32[1,12288]{1,0:T(1,128)} %bitcast.26, s32[32]{0:T(128)} %count_ref.1), custom_call_target="tpu_custom_call" | custom-call | tf_op jit(solution)/shard_map/owner_project/pallas_call | solution.py:642
  17.5 7.3 %all-to-all-start = ((f32[32,32,128]{2,1,0:T(8,128)}), f32[32,32,128]{2,1,0:T(8,128)S(1)}, u32[]{:S(2)}, u32[]{:S(2)}) async-start(f32[32,32,128]{2,1,0:T(8,128)} %get-tuple-element.12), calls=%async_computation | async-start | bytes 1048576 | tf_op jit(solution)/shard_map/all_to_all | solution.py:654
  24.8 0.0 copy-done.1
  24.9 5.3 %collective-permute-start.3 = (f32[3,10,640]{2,1,0:T(8,128)S(1)}, f32[3,10,640]{2,1,0:T(8,128)S(1)}, u32[]{:S(2)}, u32[]{:S(2)}) collective-permute-start(f32[3,10,640]{2,1,0:T(8,128)S(1)} %get-tuple-element.18), channel_id=1, source_target_pairs={{1,0},{2,1},{3,2},{4,3},{5,4},{6,5},{7,6},{8,7},{9,8},{10,9},{11,1... | collective-permute-start | bytes 230408 | tf_op jit(solution)/shard_map/ppermute | solution.py:699
  30.1 0.0 collective-permute-start.2
  30.2 0.7 tile.10.anchor_ref
  30.9 0.0 copy-done.3
  30.9 0.1 copy.21
  31.0 0.7 reshape.136.keys_ref
  31.8 0.1 pad.12.clone
  31.8 0.6 fusion.3.inside_ref
  32.4 2.9 %collective-permute-done.3 = f32[3,10,640]{2,1,0:T(8,128)S(1)} collective-permute-done((f32[3,10,640]{2,1,0:T(8,128)S(1)}, f32[3,10,640]{2,1,0:T(8,128)S(1)}, u32[]{:S(2)}, u32[]{:S(2)}) %collective-permute-start.3) | collective-permute-done | bytes 76832 | tf_op jit(solution)/shard_map/ppermute | solution.py:699
  35.3 6.4 %all-to-all-done.arrived_ref = f32[32,32,128]{2,1,0:T(8,128)S(1)} async-done(((f32[32,32,128]{2,1,0:T(8,128)}), f32[32,32,128]{2,1,0:T(8,128)S(1)}, u32[]{:S(2)}, u32[]{:S(2)}) %all-to-all-start) | async-done | bytes 524320 | tf_op jit(solution)/shard_map/all_to_all | solution.py:654
  41.7 0.0 copy-start
  41.7 0.8 copy-done
  42.5 18.5 %blend.1 = (f32[3,40,256]{2,1,0:T(8,128)}, f32[5,5120]{1,0:T(8,128)}, s32[2,5120]{1,0:T(2,128)}, f32[5120,32]{1,0:T(8,128)}) custom-call(f32[32,32,128]{2,1,0:T(8,128)} %copy-done, s32[1,5120]{1,0:T(1,128)} %reshape.136.keys_ref, f32[2,5120]{1,0:T(2,128)} %tile.10.anchor_ref, bf16[32,256]{1,0:T(8,128)(2,1)} %constant.75.clone.powers_ref), custom_call_target="tpu_custom_call" | custom-call | tf_op jit(solution)/shard_map/blend/pallas_call | solution.py:669
  60.9 1.1 copy.22
  62.0 0.3 copy.23
  62.4 0.3 reshape.138
  62.7 0.1 collective-permute-start
  62.8 0.0 collective-permute-done.2
  62.8 5.5 %collective-permute-start.1 = (f32[3,10,640]{2,1,0:T(8,128)S(1)}, f32[3,10,640]{2,1,0:T(8,128)S(1)}, u32[]{:S(2)}, u32[]{:S(2)}) collective-permute-start(f32[3,10,640]{2,1,0:T(8,128)S(1)} %get-tuple-element.20), channel_id=1, source_target_pairs={{1,0},{2,1},{3,2},{4,3},{5,4},{6,5},{7,6},{8,7},{9,8},{10,9},{11,1... | collective-permute-start | bytes 230408 | tf_op jit(solution)/shard_map/ppermute | solution.py:699
  68.3 2.4 %collective-permute-done = f32[3,10,640]{2,1,0:T(8,128)S(1)} collective-permute-done((f32[3,10,640]{2,1,0:T(8,128)S(1)}, f32[3,10,640]{2,1,0:T(8,128)S(1)}, u32[]{:S(2)}, u32[]{:S(2)}) %collective-permute-start) | collective-permute-done | bytes 76832 | tf_op jit(solution)/shard_map/ppermute | solution.py:698
  70.8 0.0 collective-permute-done.1
  70.8 0.9 maximum_maximum_fusion.1
  71.7 9.9 %window_loss.1 = f32[3,16,640]{2,1,0:T(8,128)} custom-call(f32[3,40,640]{2,1,0:T(8,128)} %get-tuple-element.22.whole_ref, f32[3,40,640]{2,1,0:T(8,128)} %get-tuple-element.21.truth_ref, f32[32,1]{1,0:T(8,128)} %fusion.3.inside_ref, f32[32,40]{1,0:T(8,128)} %constant.76.clone.down_ref, f32[16,32]{1,0:T(8,128)} %constant.77.clone.back_ref, ...), custom_call_target="tpu_custom_call" | custom-call | tf_op jit(solution)/shard_map/window_loss/pallas_call | solution.py:711
  81.7 1.2 reshape.139
  82.9 0.3 copy.25
  83.2 0.8 copy.26.grad_ref
  84.0 28.6 %blend_pull.1 = f32[32,32,128]{2,1,0:T(8,128)} custom-call(f32[3,40,256]{2,1,0:T(8,128)} %copy.26.grad_ref, f32[5,5120]{1,0:T(8,128)} %get-tuple-element.14.feet_ref, s32[2,5120]{1,0:T(2,128)} %get-tuple-element.15.place_ref, f32[5120,32]{1,0:T(8,128)} %get-tuple-element.16.columns_ref, bf16[32,256]{1,0:T(8,128)(2,1)} %constant.75.clone.powers_ref, ...), custom_call_target="tpu_custom_call" | custom-call | tf_op jit(solution)/shard_map/blend_pull/pallas_call | solution.py:726
  112.6 21.5 %all_to_all.10.returned_ref = f32[32,32,128]{2,1,0:T(8,128)} all-to-all(f32[32,32,128]{2,1,0:T(8,128)} %blend_pull.1), channel_id=1, replica_groups=mesh['strip'=32] {'strip'}, dimensions={0} | all-to-all | bytes 1048576 | tf_op jit(solution)/shard_map/all_to_all | solution.py:746
  134.2 13.7 %owner_pull.1 = f32[59,40,128]{2,1,0:T(8,128)} custom-call(f32[59,40,128]{2,1,0:T(8,128)} %slice.18.params_ref, f32[4,12]{1,0:T(4,128)} %camera_ref.3, s32[1,12288]{1,0:T(1,128)} %bitcast.27, f32[40,128]{1,0:T(8,128)} %get-tuple-element.11.view_ref, f32[32,32,128]{2,1,0:T(8,128)} %all_to_all.10.returned_ref), custom_call_target="tpu_custom_call" | custom-call | tf_op jit(solution)/shard_map/owner_pull/pallas_call | solution.py:749
  147.8 1.4 pad.15
  149.2 1.3 copy.29
  (11 shorter events, 0.1 us)
Async XLA Ops:
  1.6 1.1 copy-start.2
  2.7 22.2 %copy-start.1 = (f32[3,16,640]{2,1,0:T(8,128)S(1)}, f32[3,16,640]{2,1,0:T(8,128)}, u32[]{:S(2)}) copy-start(f32[3,16,640]{2,1,0:T(8,128)} %param.17) | copy-start | bytes 368644
  3.3 27.6 %copy-start.3 = (s32[40,128]{1,0:T(8,128)S(1)}, s32[40,128]{1,0:T(8,128)}, u32[]{:S(2)}) copy-start(s32[40,128]{1,0:T(8,128)} %param.16) | copy-start | bytes 61444
  17.5 24.2 %all-to-all-start = ((f32[32,32,128]{2,1,0:T(8,128)}), f32[32,32,128]{2,1,0:T(8,128)S(1)}, u32[]{:S(2)}, u32[]{:S(2)}) async-start(f32[32,32,128]{2,1,0:T(8,128)} %get-tuple-element.12), calls=%async_computation | async-start | bytes 1048576 | tf_op jit(solution)/shard_map/all_to_all | solution.py:654
  24.9 10.4 %collective-permute-start.3 = (f32[3,10,640]{2,1,0:T(8,128)S(1)}, f32[3,10,640]{2,1,0:T(8,128)S(1)}, u32[]{:S(2)}, u32[]{:S(2)}) collective-permute-start(f32[3,10,640]{2,1,0:T(8,128)S(1)} %get-tuple-element.18), channel_id=1, source_target_pairs={{1,0},{2,1},{3,2},{4,3},{5,4},{6,5},{7,6},{8,7},{9,8},{10,9},{11,1... | collective-permute-start | bytes 230408 | tf_op jit(solution)/shard_map/ppermute | solution.py:699
  30.1 32.6 %collective-permute-start.2 = (f32[3,10,640]{2,1,0:T(8,128)S(1)}, f32[3,10,640]{2,1,0:T(8,128)S(1)}, u32[]{:S(2)}, u32[]{:S(2)}) collective-permute-start(f32[3,10,640]{2,1,0:T(8,128)S(1)} %get-tuple-element.17), channel_id=1, source_target_pairs={{0,1},{1,2},{2,3},{3,4},{4,5},{5,6},{6,7},{7,8},{8,9},{9,10},{10,1... | collective-permute-start | bytes 230408 | tf_op jit(solution)/shard_map/ppermute | solution.py:698
  41.7 0.8 copy-start
  62.7 8.1 %collective-permute-start = (f32[3,10,640]{2,1,0:T(8,128)S(1)}, f32[3,10,640]{2,1,0:T(8,128)S(1)}, u32[]{:S(2)}, u32[]{:S(2)}) collective-permute-start(f32[3,10,640]{2,1,0:T(8,128)S(1)} %get-tuple-element.19), channel_id=1, source_target_pairs={{0,1},{1,2},{2,3},{3,4},{4,5},{5,6},{6,7},{7,8},{8,9},{9,10},{10,1... | collective-permute-start | bytes 230408 | tf_op jit(solution)/shard_map/ppermute | solution.py:698
  62.8 8.0 %collective-permute-start.1 = (f32[3,10,640]{2,1,0:T(8,128)S(1)}, f32[3,10,640]{2,1,0:T(8,128)S(1)}, u32[]{:S(2)}, u32[]{:S(2)}) collective-permute-start(f32[3,10,640]{2,1,0:T(8,128)S(1)} %get-tuple-element.20), channel_id=1, source_target_pairs={{1,0},{2,1},{3,2},{4,3},{5,4},{6,5},{7,6},{8,7},{9,8},{10,9},{11,1... | collective-permute-start | bytes 230408 | tf_op jit(solution)/shard_map/ppermute | solution.py:699
